TPU v7x, 32 devices: a whole 2x2x4 slice. The times are simulated.
32 devices in a mesh: seg: 8 (over y, x, core), band: 4 (over z).
Axes of the slice: x: 2, y: 2, z: 4, core: 2. Of those that a mesh axis runs over, the one named last changes fastest.
Arguments:
- jac_first: bfloat16 [8, 4, 4096, 384], P('seg', None, 'band'), may hold values from -0.09375 to 0.09375
- jac_second: bfloat16 [8, 4, 4096, 384], P('seg', None, 'band'), may hold values from -0.013671875 to 0.013671875
- residual: bfloat16 [8, 4, 4096], P('seg', None, 'band'), may hold values from -1.25 to 1.25
- damp_inner: float32 [8, 3, 384], P('seg'), may hold values from 0.01 to 0.05
- damp_sep: float32 [8, 384], P('seg'), may hold values from 0.01 to 0.05
Outputs:
- separators: float32 [8, 384], P('seg')
- interior: float32 [8, 3, 384], P('seg')
All inputs are finite; a program needn't handle non-finite values.
Results may differ from a plain program's by a relative error of at most 0.0003.
Values may be sent and summed in bfloat16 or wider, within the bound.
A program may use at most 128 MiB of HBM per device.

v0:
```python
import jax
import jax.numpy as jnp
from jax import lax
from jax.sharding import PartitionSpec as P

HIGH = lax.Precision.HIGHEST


def shifted_2(shard, axis, by):
    devices = lax.axis_size(axis)
    return lax.ppermute(shard, axis, [(i, (i + by) % devices) for i in range(devices)])


def matmul_high(left, right):
    return jnp.matmul(left, right, precision=HIGH)


def lower_solve(chol, rhs):
    return jax.scipy.linalg.solve_triangular(chol, rhs, lower=True)


def upper_solve(chol, rhs):
    return jax.scipy.linalg.solve_triangular(chol, rhs, lower=True, trans=1)


def link_tiles(first, second, resid):
    paa = jnp.einsum("lri,lrj->lij", first, first, preferred_element_type=jnp.float32)
    pab = jnp.einsum("lri,lrj->lij", first, second, preferred_element_type=jnp.float32)
    pbb = jnp.einsum("lri,lrj->lij", second, second, preferred_element_type=jnp.float32)
    grad_a = jnp.einsum("lri,lr->li", first, resid, preferred_element_type=jnp.float32)
    grad_b = jnp.einsum("lri,lr->li", second, resid, preferred_element_type=jnp.float32)
    size = paa.shape[-1]
    zero_tile = jnp.zeros((1, size, size), jnp.float32)
    zero_row = jnp.zeros((1, size), jnp.float32)
    diag = jnp.concatenate([paa, zero_tile]) + jnp.concatenate(
        [zero_tile, pbb - pab - jnp.swapaxes(pab, 1, 2) + paa]
    )
    off = pab - paa
    grad = jnp.concatenate([grad_a, zero_row]) + jnp.concatenate([zero_row, grad_b - grad_a])
    return (diag, off, grad)


def segment_complement(diag, off, grad, damp_inner, damp_sep):
    size = diag.shape[-1]
    inner = damp_inner.shape[0]
    chols, lows, zlist, wlist = ([], [], [], [])
    zero = jnp.zeros((size, size), jnp.float32)
    for k in range(inner):
        block = diag[k + 1] + jnp.diag(damp_inner[k])
        left = off[0].T if k == 0 else zero
        right = off[inner] if k == inner - 1 else zero
        couple = jnp.concatenate([left, right], axis=1)
        target = -grad[k + 1]
        if k > 0:
            block = block - matmul_high(lows[-1], lows[-1].T)
            couple = couple - matmul_high(lows[-1], zlist[-1])
            target = target - matmul_high(lows[-1], wlist[-1])
        chol = jnp.linalg.cholesky(block)
        zlist.append(lower_solve(chol, couple))
        wlist.append(lower_solve(chol, target))
        chols.append(chol)
        if k < inner - 1:
            lows.append(lower_solve(chol, off[k + 1]).T)
    top = jnp.concatenate([diag[0], zero], axis=1)
    bottom = jnp.concatenate([zero, diag[inner + 1] + jnp.diag(damp_sep)], axis=1)
    schur = jnp.concatenate([top, bottom], axis=0)
    reduced = jnp.concatenate([-grad[0], -grad[inner + 1]])
    for k in range(inner):
        schur = schur - matmul_high(zlist[k].T, zlist[k])
        reduced = reduced - matmul_high(zlist[k].T, wlist[k])
    comp = (
        schur[:size, :size],
        schur[:size, size:],
        schur[size:, size:],
        reduced[:size],
        reduced[size:],
    )
    return (comp, (chols, lows, zlist, wlist))


def back_substitute(factors, left, right):
    chols, lows, zlist, wlist = factors
    inner = len(chols)
    ends = jnp.concatenate([left, right])
    values = [wlist[k] - matmul_high(zlist[k], ends) for k in range(inner)]
    steps = [None] * inner
    steps[inner - 1] = upper_solve(chols[inner - 1], values[inner - 1])
    for k in range(inner - 2, -1, -1):
        steps[k] = upper_solve(chols[k], values[k] - matmul_high(lows[k].T, steps[k + 1]))
    return jnp.stack(steps)


def merge(first_arc, second_arc):
    all_a, alr_a, arr_a, al_a, ar_a = first_arc
    bll, blr, brr, bl, br = second_arc
    size = all_a.shape[0]
    chol = jnp.linalg.cholesky(arr_a + bll)
    couple = jnp.concatenate([alr_a.T, blr], axis=1)
    weights = jax.scipy.linalg.cho_solve((chol, True), couple)
    shifted = jax.scipy.linalg.cho_solve((chol, True), ar_a + bl)
    new_ll = all_a - matmul_high(alr_a, weights[:, :size])
    new_lr = -matmul_high(alr_a, weights[:, size:])
    new_rr = brr - matmul_high(blr.T, weights[:, size:])
    new_l = al_a - matmul_high(alr_a, shifted)
    new_r = br - matmul_high(blr.T, shifted)
    return ((new_ll, new_lr, new_rr, new_l, new_r), (weights, shifted))


def closure(arc):
    all_a, alr_a, arr_a, al_a, ar_a = arc
    whole = all_a + alr_a + alr_a.T + arr_a
    chol = jnp.linalg.cholesky(whole)
    return jax.scipy.linalg.cho_solve((chol, True), al_a + ar_a)


def shards(jac_first, jac_second, residual, damp_inner, damp_sep):
    diag_part, off_part, grad_part = link_tiles(jac_first[0], jac_second[0], residual[0])
    diag, off, grad = lax.psum((diag_part, off_part, grad_part), "band")
    comp, factors = segment_complement(diag, off, grad, damp_inner[0], damp_sep[0])
    count = lax.axis_size("seg")
    levels = count.bit_length() - 1
    arc = comp
    saved_all = []
    for level in range(levels):
        neighbour = shifted_2((arc[0], arc[1], arc[2], arc[3], arc[4]), "seg", 1 << level)
        arc, saved = merge(neighbour, arc)
        saved_all.append(saved)
    top = closure(arc)
    left = shifted_2(top, "seg", 1)
    interior = back_substitute(factors, left, top)
    return (top[None], interior[None])


def solution(mesh):
    return jax.shard_map(
        shards,
        mesh=mesh,
        in_specs=(
            P("seg", None, "band", None),
            P("seg", None, "band", None),
            P("seg", None, "band"),
            P("seg", None, None),
            P("seg", None),
        ),
        out_specs=(P("seg", None), P("seg", None, None)),
        check_vma=False,
    )
```

profile of v0, /device:TPU:0, one launch (start us, length us, event | category | flops | bytes accessed | tf_op | source)
XLA Modules:
  0.0 1123.4 jit_solution(11412804855511353208)
XLA Ops:
  37.7 25.7 %psum.23 = f32[5,384]{1,0:T(8,128)S(1)} all-reduce(f32[5,384]{1,0:T(8,128)S(1)} %pad_add_fusion.1), channel_id=1, replica_groups=mesh['seg'=8,'band'=4] {'band'}, use_global_device_ids=true, to_apply=%region_8.13 | all-reduce | flops 1920 | bytes 15360 | tf_op jit(solution)/shard_map/psum | solution.py:118
  64.0 164.5 %all-reduce.12.cloned.1.call-done = (f32[4,384,384]{2,1,0:T(8,128)}, f32[5,384,384]{1,2,0:T(8,128)}) async-done(((f32[4,384,384]{2,1,0:T(8,128)}, f32[5,384,384]{1,2,0:T(8,128)}), (f32[4,384,384]{2,1,0:T(8,128)}, f32[5,384,384]{1,2,0:T(8,128)})) %all-reduce.12.cloned.1.call-update) | async-done | bytes 5308432 | tf_op jit(solution)/shard_map/psum | solution.py:118
  233.6 11.7 %cholesky.533 = f32[128,128]{1,0:T(8,128)S(1)} custom-call(f32[128,128]{1,0:T(8,128)S(1)} %cholesky.900), custom_call_target="Cholesky" | custom-call | tf_op jit(solution)/shard_map/jit(cholesky)/cholesky | solution.py:58
  256.5 11.7 %cholesky.552 = f32[128,128]{1,0:T(8,128)S(1)} custom-call(f32[128,128]{1,0:T(8,128)S(1)} %cholesky.904), custom_call_target="Cholesky" | custom-call | tf_op jit(solution)/shard_map/jit(cholesky)/cholesky | solution.py:58
  268.9 10.3 custom-call.65
  279.7 11.7 %cholesky.571 = f32[128,128]{1,0:T(8,128)S(1)} custom-call(f32[128,128]{1,0:T(8,128)S(1)} %convolution_subtract_fusion.31), custom_call_target="Cholesky" | custom-call | tf_op jit(solution)/shard_map/jit(cholesky)/cholesky | solution.py:58
  300.5 29.7 %custom-call.66 = f32[3,128,128]{1,2,0:T(8,128)S(1)} custom-call(f32[3,128,128]{2,1,0:T(8,128)S(1)} %get-tuple-element.171), custom_call_target="InvertDiagBlocksLowerTriangular" | custom-call | tf_op jit(solution)/shard_map/jit(_solve_triangular)/triangular_solve/custom-call.1 | solution.py:19
  348.6 11.7 %cholesky.586 = f32[128,128]{1,0:T(8,128)S(1)} custom-call(f32[128,128]{1,0:T(8,128)S(1)} %cholesky.908), custom_call_target="Cholesky" | custom-call | tf_op jit(solution)/shard_map/jit(cholesky)/cholesky | solution.py:58
  373.3 11.7 %cholesky.605 = f32[128,128]{1,0:T(8,128)S(1)} custom-call(f32[128,128]{1,0:T(8,128)S(1)} %cholesky.912), custom_call_target="Cholesky" | custom-call | tf_op jit(solution)/shard_map/jit(cholesky)/cholesky | solution.py:58
  397.2 11.7 %cholesky.624 = f32[128,128]{1,0:T(8,128)S(1)} custom-call(f32[128,128]{1,0:T(8,128)S(1)} %convolution_subtract_fusion.30), custom_call_target="Cholesky" | custom-call | tf_op jit(solution)/shard_map/jit(cholesky)/cholesky | solution.py:58
  417.9 29.7 %custom-call.70 = f32[3,128,128]{1,2,0:T(8,128)S(1)} custom-call(f32[3,128,128]{2,1,0:T(8,128)S(1)} %get-tuple-element.173), custom_call_target="InvertDiagBlocksLowerTriangular" | custom-call | tf_op jit(solution)/shard_map/jit(_solve_triangular)/triangular_solve/custom-call.1 | solution.py:19
  456.4 11.7 %cholesky.639 = f32[128,128]{1,0:T(8,128)S(1)} custom-call(f32[128,128]{1,0:T(8,128)S(1)} %cholesky.916), custom_call_target="Cholesky" | custom-call | tf_op jit(solution)/shard_map/jit(cholesky)/cholesky | solution.py:58
  480.4 11.9 %cholesky.658 = f32[128,128]{1,0:T(8,128)S(1)} custom-call(f32[128,128]{1,0:T(8,128)S(1)} %cholesky.920), custom_call_target="Cholesky" | custom-call | tf_op jit(solution)/shard_map/jit(cholesky)/cholesky | solution.py:58
  503.5 11.7 %cholesky.677 = f32[128,128]{1,0:T(8,128)S(1)} custom-call(f32[128,128]{1,0:T(8,128)S(1)} %convolution_subtract_fusion.29), custom_call_target="Cholesky" | custom-call | tf_op jit(solution)/shard_map/jit(cholesky)/cholesky | solution.py:58
  526.1 30.0 %custom-call.74 = f32[3,128,128]{1,2,0:T(8,128)S(1)} custom-call(f32[3,128,128]{2,1,0:T(8,128)S(1)} %get-tuple-element.175), custom_call_target="InvertDiagBlocksLowerTriangular" | custom-call | tf_op jit(solution)/shard_map/jit(_solve_triangular)/triangular_solve/custom-call.1 | solution.py:19
  589.2 11.7 %cholesky.692 = f32[128,128]{1,0:T(8,128)S(1)} custom-call(f32[128,128]{1,0:T(8,128)S(1)} %cholesky.924), custom_call_target="Cholesky" | custom-call | tf_op jit(solution)/shard_map/jit(cholesky)/cholesky | solution.py:97
  612.1 11.7 %cholesky.711 = f32[128,128]{1,0:T(8,128)S(1)} custom-call(f32[128,128]{1,0:T(8,128)S(1)} %cholesky.928), custom_call_target="Cholesky" | custom-call | tf_op jit(solution)/shard_map/jit(cholesky)/cholesky | solution.py:97
  635.2 11.7 %cholesky.730 = f32[128,128]{1,0:T(8,128)S(1)} custom-call(f32[128,128]{1,0:T(8,128)S(1)} %slice_subtract_fusion.5), custom_call_target="Cholesky" | custom-call | tf_op jit(solution)/shard_map/jit(cholesky)/cholesky | solution.py:97
  656.0 29.5 %custom-call.77 = f32[3,128,128]{1,2,0:T(8,128)S(1)} custom-call(f32[3,128,128]{2,1,0:T(8,128)S(1)} %get-tuple-element.176), custom_call_target="InvertDiagBlocksLowerTriangular" | custom-call | tf_op jit(solution)/shard_map/jit(_cho_solve)/triangular_solve | solution.py:99
  731.0 11.7 %cholesky.745 = f32[128,128]{1,0:T(8,128)S(1)} custom-call(f32[128,128]{1,0:T(8,128)S(1)} %cholesky.932), custom_call_target="Cholesky" | custom-call | tf_op jit(solution)/shard_map/jit(cholesky)/cholesky | solution.py:97
  753.9 11.7 %cholesky.764 = f32[128,128]{1,0:T(8,128)S(1)} custom-call(f32[128,128]{1,0:T(8,128)S(1)} %cholesky.936), custom_call_target="Cholesky" | custom-call | tf_op jit(solution)/shard_map/jit(cholesky)/cholesky | solution.py:97
  776.9 11.7 %cholesky.783 = f32[128,128]{1,0:T(8,128)S(1)} custom-call(f32[128,128]{1,0:T(8,128)S(1)} %slice_subtract_fusion.4), custom_call_target="Cholesky" | custom-call | tf_op jit(solution)/shard_map/jit(cholesky)/cholesky | solution.py:97
  797.4 29.7 %custom-call.81 = f32[3,128,128]{1,2,0:T(8,128)S(1)} custom-call(f32[3,128,128]{2,1,0:T(8,128)S(1)} %get-tuple-element.178), custom_call_target="InvertDiagBlocksLowerTriangular" | custom-call | tf_op jit(solution)/shard_map/jit(_cho_solve)/triangular_solve | solution.py:99
  850.6 26.9 %collective-permute-done.8 = f32[384,384]{0,1:T(8,128)S(1)} collective-permute-done((f32[384,384]{0,1:T(8,128)}, f32[384,384]{0,1:T(8,128)S(1)}, u32[]{:S(2)}, u32[]{:S(2)}) %collective-permute-start.8) | collective-permute-done | bytes 589856 | tf_op jit(solution)/shard_map/ppermute | solution.py:11
  878.7 11.7 %cholesky.798 = f32[128,128]{1,0:T(8,128)S(1)} custom-call(f32[128,128]{1,0:T(8,128)S(1)} %cholesky.940), custom_call_target="Cholesky" | custom-call | tf_op jit(solution)/shard_map/jit(cholesky)/cholesky | solution.py:97
  901.5 12.1 %cholesky.817 = f32[128,128]{1,0:T(8,128)S(1)} custom-call(f32[128,128]{1,0:T(8,128)S(1)} %cholesky.944), custom_call_target="Cholesky" | custom-call | tf_op jit(solution)/shard_map/jit(cholesky)/cholesky | solution.py:97
  924.7 11.7 %cholesky.836 = f32[128,128]{1,0:T(8,128)S(1)} custom-call(f32[128,128]{1,0:T(8,128)S(1)} %slice_subtract_fusion.3), custom_call_target="Cholesky" | custom-call | tf_op jit(solution)/shard_map/jit(cholesky)/cholesky | solution.py:97
  945.0 29.7 %custom-call.85 = f32[3,128,128]{1,2,0:T(8,128)S(1)} custom-call(f32[3,128,128]{2,1,0:T(8,128)S(1)} %get-tuple-element.180), custom_call_target="InvertDiagBlocksLowerTriangular" | custom-call | tf_op jit(solution)/shard_map/jit(_cho_solve)/triangular_solve | solution.py:99
  998.5 11.7 %cholesky.851 = f32[128,128]{1,0:T(8,128)S(1)} custom-call(f32[128,128]{1,0:T(8,128)S(1)} %cholesky.948), custom_call_target="Cholesky" | custom-call | tf_op jit(solution)/shard_map/jit(cholesky)/cholesky | solution.py:112
  1021.4 11.7 %cholesky.870 = f32[128,128]{1,0:T(8,128)S(1)} custom-call(f32[128,128]{1,0:T(8,128)S(1)} %cholesky.952), custom_call_target="Cholesky" | custom-call | tf_op jit(solution)/shard_map/jit(cholesky)/cholesky | solution.py:112
  1044.4 11.7 %cholesky.889 = f32[128,128]{1,0:T(8,128)S(1)} custom-call(f32[128,128]{1,0:T(8,128)S(1)} %convolution_subtract_fusion.28), custom_call_target="Cholesky" | custom-call | tf_op jit(solution)/shard_map/jit(cholesky)/cholesky | solution.py:112
  1064.9 29.5 %custom-call.99 = f32[3,128,128]{1,2,0:T(8,128)S(1)} custom-call(f32[3,128,128]{2,1,0:T(8,128)S(1)} %get-tuple-element.192), custom_call_target="InvertDiagBlocksLowerTriangular" | custom-call | tf_op jit(solution)/shard_map/jit(_cho_solve)/triangular_solve/custom-call.7 | solution.py:113
  (641 shorter events, 453.9 us)
Async XLA Ops:
  7.2 221.3 %all-reduce.12.cloned.1.call-start = ((), (), s32[]{:S(2)}) async-start(), calls=%async_computation | async-start | bytes 10616832 | tf_op jit(solution)/shard_map/psum | solution.py:118
  333.5 241.0 %copy-start.4 = (f32[128,768]{1,0:T(8,128)}, f32[128,768]{1,0:T(8,128)S(1)}, u32[]{:S(2)}) copy-start(f32[128,768]{1,0:T(8,128)S(1)} %fusion.131) | copy-start | bytes 1179652
  417.9 140.5 %copy-start.16 = (f32[384,384]{1,0:T(8,128)}, f32[384,384]{1,0:T(8,128)S(1)}, u32[]{:S(2)}) copy-start(f32[384,384]{1,0:T(8,128)S(1)} %get-tuple-element.684) | copy-start | bytes 1769476
  447.5 111.4 %copy-start.33 = (f32[3,128,128]{1,2,0:T(8,128)}, f32[3,128,128]{1,2,0:T(8,128)S(1)}, u32[]{:S(2)}) copy-start(f32[3,128,128]{1,2,0:T(8,128)S(1)} %custom-call.70) | copy-start | bytes 589828
  526.1 41.2 %copy-start.18 = (f32[384,384]{1,0:T(8,128)}, f32[384,384]{1,0:T(8,128)S(1)}, u32[]{:S(2)}) copy-start(f32[384,384]{1,0:T(8,128)S(1)} %get-tuple-element.689) | copy-start | bytes 1769476
  574.4 11.1 collective-permute-start.2
  577.6 7.4 collective-permute-start.10
  585.5 123.6 %collective-permute-start.9 = (f32[384]{0:T(512)}, f32[384]{0:T(512)}, u32[]{:S(2)}, u32[]{:S(2)}) collective-permute-start(f32[384]{0:T(512)} %get-tuple-element.342), channel_id=1, source_target_pairs={{0,4},{4,8},{8,12},{12,16},{16,20},{20,24},{24,28},{28,0},{1,5},{5... | collective-permute-start | bytes 4616 | tf_op jit(solution)/shard_map/ppermute | solution.py:11
  688.2 10.4 collective-permute-start.1
  691.0 18.2 %collective-permute-start.12 = (f32[384]{0:T(512)S(1)}, f32[384]{0:T(512)S(1)}, u32[]{:S(2)}, u32[]{:S(2)}) collective-permute-start(f32[384]{0:T(512)S(1)} %slice_subtract_fusion.22), channel_id=1, source_target_pairs={{0,8},{4,12},{8,16},{12,20},{16,24},{20,28},{24,0},{28,4},{1,9},{5... | collective-permute-start | bytes 4616 | tf_op jit(solution)/shard_map/ppermute | solution.py:11
  693.4 23.1 %collective-permute-start = (f32[384,384]{0,1:T(8,128)}, f32[384,384]{0,1:T(8,128)}, u32[]{:S(2)}, u32[]{:S(2)}) collective-permute-start(f32[384,384]{0,1:T(8,128)} %get-tuple-element.285), channel_id=1, source_target_pairs={{0,4},{4,8},{8,12},{12,16},{16,20},{20,24},{24,28},{28,0},{1,5},{5... | collective-permute-start | bytes 1769480 | tf_op jit(solution)/shard_map/ppermute | solution.py:11
  708.5 17.5 %collective-permute-start.5 = (f32[384,384]{0,1:T(8,128)}, f32[384,384]{0,1:T(8,128)}, u32[]{:S(2)}, u32[]{:S(2)}) collective-permute-start(f32[384,384]{0,1:T(8,128)} %convolution_subtract_fusion.4), channel_id=1, source_target_pairs={{0,8},{4,12},{8,16},{12,20},{16,24},{20,28},{24,0},{28,4},{1,9},{5... | collective-permute-start | bytes 1769480 | tf_op jit(solution)/shard_map/ppermute | solution.py:11
  711.0 137.2 %collective-permute-start.11 = (f32[384]{0:T(512)}, f32[384]{0:T(512)}, u32[]{:S(2)}, u32[]{:S(2)}) collective-permute-start(f32[384]{0:T(512)} %get-tuple-element.266), channel_id=1, source_target_pairs={{0,8},{4,12},{8,16},{12,20},{16,24},{20,28},{24,0},{28,4},{1,9},{5... | collective-permute-start | bytes 4616 | tf_op jit(solution)/shard_map/ppermute | solution.py:11
  716.3 115.5 %collective-permute-start.4 = (f32[384,384]{1,0:T(8,128)}, f32[384,384]{1,0:T(8,128)S(1)}, u32[]{:S(2)}, u32[]{:S(2)}) collective-permute-start(f32[384,384]{1,0:T(8,128)} %copy.22), channel_id=1, source_target_pairs={{0,8},{4,12},{8,16},{12,20},{16,24},{20,28},{24,0},{28,4},{1,9},{5... | collective-permute-start | bytes 1769480 | tf_op jit(solution)/shard_map/ppermute | solution.py:11
  788.7 38.4 %copy-start.71 = (f32[384,1]{0,1:T(1,128)S(1)}, f32[384,1]{0,1:T(1,128)}, u32[]{:S(2)}) copy-start(f32[384,1]{0,1:T(1,128)} %broadcast_in_dim.100) | copy-start | bytes 4612
  791.4 38.4 %copy-start.66 = (f32[384]{0:T(512)S(1)}, f32[384]{0:T(512)}, u32[]{:S(2)}) copy-start(f32[384]{0:T(512)} %copy-done.65) | copy-start | bytes 4612
  830.4 17.8 %collective-permute-start.14 = (f32[384]{0:T(512)}, f32[384]{0:T(512)}, u32[]{:S(2)}, u32[]{:S(2)}) collective-permute-start(f32[384]{0:T(512)} %sub.124), channel_id=1, source_target_pairs={{0,16},{4,20},{8,24},{12,28},{16,0},{20,4},{24,8},{28,12},{1,17},{... | collective-permute-start | bytes 4616 | tf_op jit(solution)/shard_map/ppermute | solution.py:11
  843.9 133.4 %collective-permute-start.7 = (f32[384,384]{1,0:T(8,128)}, f32[384,384]{1,0:T(8,128)S(1)}, u32[]{:S(2)}, u32[]{:S(2)}) collective-permute-start(f32[384,384]{1,0:T(8,128)} %copy.26), channel_id=1, source_target_pairs={{0,16},{4,20},{8,24},{12,28},{16,0},{20,4},{24,8},{28,12},{1,17},{... | collective-permute-start | bytes 1769480 | tf_op jit(solution)/shard_map/ppermute | solution.py:11
  844.4 33.0 %collective-permute-start.8 = (f32[384,384]{0,1:T(8,128)}, f32[384,384]{0,1:T(8,128)S(1)}, u32[]{:S(2)}, u32[]{:S(2)}) collective-permute-start(f32[384,384]{0,1:T(8,128)} %convolution_subtract_fusion.3), channel_id=1, source_target_pairs={{0,16},{4,20},{8,24},{12,28},{16,0},{20,4},{24,8},{28,12},{1,17},{... | collective-permute-start | bytes 1769480 | tf_op jit(solution)/shard_map/ppermute | solution.py:11
  845.9 31.6 %collective-permute-start.3 = (f32[384,384]{0,1:T(8,128)}, f32[384,384]{0,1:T(8,128)S(1)}, u32[]{:S(2)}, u32[]{:S(2)}) collective-permute-start(f32[384,384]{0,1:T(8,128)} %get-tuple-element.355), channel_id=1, source_target_pairs={{0,8},{4,12},{8,16},{12,20},{16,24},{20,28},{24,0},{28,4},{1,9},{5... | collective-permute-start | bytes 1769480 | tf_op jit(solution)/shard_map/ppermute | solution.py:11
  850.0 137.5 %collective-permute-start.13 = (f32[384]{0:T(512)}, f32[384]{0:T(512)}, u32[]{:S(2)}, u32[]{:S(2)}) collective-permute-start(f32[384]{0:T(512)} %get-tuple-element.264), channel_id=1, source_target_pairs={{0,16},{4,20},{8,24},{12,28},{16,0},{20,4},{24,8},{28,12},{1,17},{... | collective-permute-start | bytes 4616 | tf_op jit(solution)/shard_map/ppermute | solution.py:11
  983.8 13.0 %collective-permute-start.6 = (f32[384,384]{0,1:T(8,128)}, f32[384,384]{0,1:T(8,128)}, u32[]{:S(2)}, u32[]{:S(2)}) collective-permute-start(f32[384,384]{0,1:T(8,128)} %get-tuple-element.268), channel_id=1, source_target_pairs={{0,16},{4,20},{8,24},{12,28},{16,0},{20,4},{24,8},{28,12},{1,17},{... | collective-permute-start | bytes 1769480 | tf_op jit(solution)/shard_map/ppermute | solution.py:11
  1056.1 38.3 %copy-start.72 = (f32[384,1]{0,1:T(1,128)S(1)}, f32[384,1]{0,1:T(1,128)}, u32[]{:S(2)}) copy-start(f32[384,1]{0,1:T(1,128)} %broadcast_in_dim.102) | copy-start | bytes 4612
  1058.9 38.3 %copy-start.76 = (f32[128,1]{0,1:T(1,128)S(1)}, f32[128,1]{0,1:T(1,128)}, u32[]{:S(2)}) copy-start(f32[128,1]{0,1:T(1,128)} %copy-done.74) | copy-start | bytes 1540
  1058.9 38.3 %copy-start.79 = (f32[128,1]{0,1:T(1,128)S(1)}, f32[128,1]{0,1:T(1,128)}, u32[]{:S(2)}) copy-start(f32[128,1]{0,1:T(1,128)} %copy-done.77) | copy-start | bytes 1540
  1058.9 38.3 %copy-start.87 = (f32[128,1]{0,1:T(1,128)S(1)}, f32[128,1]{0,1:T(1,128)}, u32[]{:S(2)}) copy-start(f32[128,1]{0,1:T(1,128)} %copy-done.85) | copy-start | bytes 1540
  1058.9 38.3 %copy-start.90 = (f32[128,1]{0,1:T(1,128)S(1)}, f32[128,1]{0,1:T(1,128)}, u32[]{:S(2)}) copy-start(f32[128,1]{0,1:T(1,128)} %copy-done.88) | copy-start | bytes 1540
  1058.9 42.1 %copy-start.8 = (f32[128,768]{1,0:T(8,128)S(1)}, f32[128,768]{1,0:T(8,128)}, u32[]{:S(2)}) copy-start(f32[128,768]{1,0:T(8,128)} %copy-done.7) | copy-start | bytes 1179652
  1058.9 42.1 %copy-start.20 = (f32[128,768]{1,0:T(8,128)S(1)}, f32[128,768]{1,0:T(8,128)}, u32[]{:S(2)}) copy-start(f32[128,768]{1,0:T(8,128)} %copy-done.19) | copy-start | bytes 1179652
  1064.9 38.4 %copy-start.10 = (f32[128,768]{1,0:T(8,128)S(1)}, f32[128,768]{1,0:T(8,128)}, u32[]{:S(2)}) copy-start(f32[128,768]{1,0:T(8,128)} %copy-done.9) | copy-start | bytes 1179652
  1064.9 38.4 %copy-start.22 = (f32[128,768]{1,0:T(8,128)S(1)}, f32[128,768]{1,0:T(8,128)}, u32[]{:S(2)}) copy-start(f32[128,768]{1,0:T(8,128)} %copy-done.21) | copy-start | bytes 1179652
  1097.0 4.1 collective-permute-start.15
  (79 other events, 683.7 us)
Sparse Core Ops, SparseCore 0:
  34.0 194.4 all-reduce.11
where the time goes:
time: 1130 us; the launch traced here: 1120 us
  other arithmetic  624 us (55%)
  waiting for transfers between devices  220 us (19%)
  matrix products  137 us (12%)
  local copies, waits for them, and re-layouts  71.6 us (6%)
  between operations  30.5 us (3%)
  blocking collectives  25.7 us (2%)
  starting transfers between devices  13.7 us (1%)
    another operation x33, other arithmetic, merge(): chol = jnp.linalg.cholesky(arr_a + bll)  172 us
    another operation x32, other arithmetic, segment_complement(): chol = jnp.linalg.cholesky(block)  171 us
    psum x1, waiting for transfers between devices, shards(): diag, off, grad = lax.psum((diag_part, off_part, grad_part), 'band')  164 us
    another operation x9, other arithmetic, lower_solve(): return jax.scipy.linalg.solve_triangular(chol, rhs, lower=True)  90.6 us
    another operation x9, other arithmetic, merge(): weights = jax.scipy.linalg.cho_solve((chol, True), couple)  89.2 us
    another operation x11, other arithmetic, closure(): chol = jnp.linalg.cholesky(whole)  57.2 us
    ppermute x16, waiting for transfers between devices, shifted_2(): lax.ppermute(shard, axis, [(i, (i + by) % devices) for i in range(devices)])  55.5 us
    dot_general x32, matrix products, matmul_high(): return jnp.matmul(left, right, precision=HIGH)  55.3 us
  transfers between devices with their start and end apart: 17, of which 7 were waited for; matrix products, arithmetic and copies ran while one was open for 31% of the time, Pallas kernels for 0%

commit v1 on v0

v1 whole, which is shorter than its diff:
```python
import functools

import jax
import jax.numpy as jnp
from jax import lax
from jax.experimental import pallas as pl
from jax.experimental.pallas import tpu as pltpu
from jax.sharding import PartitionSpec as P

HIGH = lax.Precision.HIGHEST
F32 = jnp.float32
BF16 = jnp.bfloat16
COARSE_STEPS = 8
FINE_STEPS = 64
FINE_ENOUGH = 1e-5
PAD = 8
VMEM_BYTES = 48 * 1024 * 1024


def mm(left, right):
    return jnp.dot(left, right, preferred_element_type=F32)


def mm_high(left, right):
    return jnp.dot(left, right, precision=HIGH, preferred_element_type=F32)


def mm_high_t(left, right):
    return lax.dot_general(
        left, right, (((1,), (1,)), ((), ())), precision=HIGH, preferred_element_type=F32
    )


def eye_mask(size):
    rows = lax.broadcasted_iota(jnp.int32, (size, size), 0)
    columns = lax.broadcasted_iota(jnp.int32, (size, size), 1)
    return rows == columns


def plus_diagonal(matrix, row):
    return matrix + jnp.where(eye_mask(matrix.shape[0]), row, 0.0)


def invert(mats, invs, resids):
    size = mats[0].shape[0]

    def start(m, x):
        scale = 1.0 / jnp.max(jnp.sum(jnp.abs(m[...]), axis=0, keepdims=True))
        x[...] = jnp.where(eye_mask(size), 2.0 * scale, 0.0) - (scale * scale) * m[...]

    def residual(m, x, r):
        r[...] = jnp.where(eye_mask(size), 1.0, 0.0) - mm_high(m[...], x[...])
        return jnp.sum(r[...] * r[...])

    def residuals():
        worst = None
        for m, x, r in zip(mats, invs, resids):
            one = residual(m, x, r)
            worst = one if worst is None else jnp.maximum(worst, one)
        return worst

    for m, x in zip(mats, invs):
        start(m, x)

    @pl.loop(0, COARSE_STEPS)
    def _(_):
        for m, x in zip(mats, invs):
            xb = x[...].astype(BF16)
            rb = jnp.where(eye_mask(size), 1.0, 0.0) - mm(m[...].astype(BF16), xb)
            x[...] += mm(xb, rb.astype(BF16))

    rho = residuals()
    good = rho < 0.25

    def keep():
        return rho

    def restart():
        for m, x in zip(mats, invs):
            start(m, x)
        return residuals()

    rho = lax.cond(good, keep, restart)

    def more(state):
        step, now = state
        return jnp.logical_and(step < FINE_STEPS, now > FINE_ENOUGH)

    def fine(state):
        step, _ = state
        for x, r in zip(invs, resids):
            x[...] += mm_high(x[...], r[...])
        return (step + 1, residuals())

    lax.while_loop(more, fine, (jnp.int32(0), rho))
    for x, r in zip(invs, resids):
        x[...] += mm_high(x[...], r[...])


def eliminate(inv, z, y, size):
    y[...] = mm_high(z[...], inv[...])
    ll = mm_high_t(y[:size, :], z[:size, :])
    lr = mm_high_t(y[:size, :], z[size : 2 * size, :])
    rr = mm_high_t(y[size : 2 * size, :], z[size : 2 * size, :])
    ends = mm_high_t(y[2 * size :, :], z[: 2 * size, :])
    return ll, lr, rr, ends[:1, :size], ends[:1, size:]


def put_couplings(z, from_left, from_right, target, size):
    z[:size, :] = from_left
    z[size : 2 * size, :] = from_right
    z[2 * size :, :] = jnp.zeros((PAD, size), F32)
    z[2 * size : 2 * size + 1, :] = target


def gram_kernel(first_ref, second_ref, resid_ref, out_ref, *, links, size):
    link = pl.program_id(0)
    first = first_ref[0]
    second = second_ref[0]
    both = jnp.concatenate([first, second], axis=1)
    at = first.T
    prod = mm(at, both)
    paa = prod[:, :size]
    pab = prod[:, size:]
    pbb = mm(second.T, second)
    grads = mm(resid_ref[0], both)[:1, :]
    grad_a = grads[:, :size]
    grad_b = grads[:, size:]
    tail = (2 * links + 1) * size

    @pl.when(link == 0)
    def _():
        out_ref[:size, :] = jnp.zeros((size, size), F32)
        out_ref[tail:, :] = jnp.zeros((PAD, size), F32)

    here = pl.multiple_of(link * size, size)
    out_ref[pl.ds(here, size), :] += paa
    out_ref[pl.ds(pl.multiple_of(here + size, size), size), :] = pbb - pab - pab.T + paa
    out_ref[pl.ds(pl.multiple_of(here + (links + 1) * size, size), size), :] = pab - paa
    rows = lax.broadcasted_iota(jnp.int32, (PAD, size), 0)
    out_ref[tail:, :] += jnp.where(rows == link, grad_a, 0.0) + jnp.where(
        rows == link + 1, grad_b - grad_a, 0.0
    )


def gram(first, second, resid):
    links, rows, size = first.shape
    height = (2 * links + 1) * size + PAD
    padded = jnp.broadcast_to(resid[:, None, :], (links, 16, rows))
    block = pl.BlockSpec((1, rows, size), lambda link: (link, 0, 0))
    return pl.pallas_call(
        functools.partial(gram_kernel, links=links, size=size),
        grid=(links,),
        in_specs=[block, block, pl.BlockSpec((1, 16, rows), lambda link: (link, 0, 0))],
        out_specs=pl.BlockSpec((height, size), lambda link: (0, 0)),
        out_shape=jax.ShapeDtypeStruct((height, size), F32),
        compiler_params=pltpu.CompilerParams(vmem_limit_bytes=VMEM_BYTES),
        name="gram",
    )(first, second, padded)


def segment_kernel(
    tiles_ref, inner_ref, sep_ref, arc_ref, y1_ref, y2_ref, y3_ref, m1, m3, x1, x3, r1, r3, z1, z3
):
    size = tiles_ref.shape[1]

    def tile(k):
        return tiles_ref[k * size : (k + 1) * size, :]

    def target(k):
        return -tiles_ref[9 * size + k : 9 * size + k + 1, :]

    m1[...] = plus_diagonal(tile(1), inner_ref[0:1, :])
    m3[...] = plus_diagonal(tile(3), inner_ref[2:3, :])
    put_couplings(z1, tile(5), tile(6).T, target(1), size)
    put_couplings(z3, tile(7), tile(8).T, target(3), size)
    invert([m1, m3], [x1, x3], [r1, r3])
    ll1, lr1, rr1, l1, e1 = eliminate(x1, z1, y1_ref, size)
    m1[...] = plus_diagonal(tile(2), inner_ref[1:2, :]) - rr1
    z1[:size, :] = -lr1
    arc_ref[:size, :] = tile(0) - ll1
    ll3, lr3, rr3, l3, e3 = eliminate(x3, z3, y3_ref, size)
    m1[...] -= ll3
    put_couplings(z1, z1[:size, :], -lr3.T, target(2) - e1 - l3, size)
    arc_ref[2 * size : 3 * size, :] = plus_diagonal(tile(4), sep_ref[0:1, :]) - rr3
    invert([m1], [x1], [r1])
    ll2, lr2, rr2, l2, e2 = eliminate(x1, z1, y2_ref, size)
    arc_ref[:size, :] -= ll2
    arc_ref[size : 2 * size, :] = -lr2
    arc_ref[2 * size : 3 * size, :] -= rr2
    arc_ref[3 * size :, :] = jnp.zeros((PAD, size), F32)
    arc_ref[3 * size : 3 * size + 1, :] = target(0) - l1 - l2
    arc_ref[3 * size + 1 : 3 * size + 2, :] = target(4) - e3 - e2


def segment(tiles, inner, sep):
    size = tiles.shape[1]
    square = pltpu.VMEM((size, size), F32)
    couplings = jax.ShapeDtypeStruct((2 * size + PAD, size), F32)
    tall = pltpu.VMEM((2 * size + PAD, size), F32)
    return pl.pallas_call(
        segment_kernel,
        out_shape=[jax.ShapeDtypeStruct((3 * size + PAD, size), F32)] + [couplings] * 3,
        scratch_shapes=[square] * 6 + [tall] * 2,
        compiler_params=pltpu.CompilerParams(vmem_limit_bytes=VMEM_BYTES),
        name="segment",
    )(tiles, inner, sep)


def merge_kernel(right_ref, mine_ref, other_ref, arc_ref, y_ref, m, x, r, z):
    size = mine_ref.shape[1]
    is_right = right_ref[0] == 1

    def first(low, high):
        return jnp.where(is_right, other_ref[low:high, :], mine_ref[low:high, :])

    def second(low, high):
        return jnp.where(is_right, mine_ref[low:high, :], other_ref[low:high, :])

    end = 3 * size
    m[...] = first(2 * size, end) + second(0, size)
    put_couplings(
        z,
        first(size, 2 * size),
        second(size, 2 * size).T,
        first(end + 1, end + 2) + second(end, end + 1),
        size,
    )
    invert([m], [x], [r])
    ll, lr, rr, left, right = eliminate(x, z, y_ref, size)
    arc_ref[:size, :] = first(0, size) - ll
    arc_ref[size : 2 * size, :] = -lr
    arc_ref[2 * size : end, :] = second(2 * size, end) - rr
    arc_ref[end:, :] = jnp.zeros((PAD, size), F32)
    arc_ref[end : end + 1, :] = first(end, end + 1) - left
    arc_ref[end + 1 : end + 2, :] = second(end + 1, end + 2) - right


def merge(is_right, mine, other):
    size = mine.shape[1]
    square = pltpu.VMEM((size, size), F32)
    vmem = pl.BlockSpec(memory_space=pltpu.VMEM)
    return pl.pallas_call(
        merge_kernel,
        in_specs=[pl.BlockSpec(memory_space=pltpu.SMEM), vmem, vmem],
        out_shape=[
            jax.ShapeDtypeStruct((3 * size + PAD, size), F32),
            jax.ShapeDtypeStruct((2 * size + PAD, size), F32),
        ],
        scratch_shapes=[square] * 3 + [pltpu.VMEM((2 * size + PAD, size), F32)],
        compiler_params=pltpu.CompilerParams(vmem_limit_bytes=VMEM_BYTES),
        name="merge",
    )(is_right, mine, other)


def finish_kernel(levels, bits_ref, arc_ref, *refs):
    merged = refs[:levels]
    y1_ref, y2_ref, y3_ref, sep_ref, inner_ref, m, x, r = refs[levels:]
    size = arc_ref.shape[1]
    end = 3 * size
    lr = arc_ref[size : 2 * size, :]
    m[...] = arc_ref[:size, :] + lr + lr.T + arc_ref[2 * size : end, :]
    invert([m], [x], [r])

    def middle(y_ref, left, right):
        return (
            y_ref[2 * size : 2 * size + PAD, :]
            - mm_high(left, y_ref[:size, :])
            - mm_high(right, y_ref[size : 2 * size, :])
        )

    total = arc_ref[end : end + 1, :] + arc_ref[end + 1 : end + 2, :]
    top = mm_high(jnp.broadcast_to(total, (PAD, size)), x[...])
    left, right = top, top
    for level in range(levels - 1, -1, -1):
        between = middle(merged[level], left, right)
        between = jnp.broadcast_to(between[:1, :], (PAD, size))
        in_right = bits_ref[level] == 1
        left, right = jnp.where(in_right, between, left), jnp.where(in_right, right, between)
    step2 = jnp.broadcast_to(middle(y2_ref, left, right)[:1, :], (PAD, size))
    step1 = middle(y1_ref, left, step2)
    step3 = middle(y3_ref, step2, right)
    sep_ref[...] = right[:1, :]
    inner_ref[0:1, :] = step1[:1, :]
    inner_ref[1:2, :] = step2[:1, :]
    inner_ref[2:3, :] = step3[:1, :]


def finish(bits, arc, merged, inner):
    size = arc.shape[1]
    square = pltpu.VMEM((size, size), F32)
    vmem = pl.BlockSpec(memory_space=pltpu.VMEM)
    return pl.pallas_call(
        functools.partial(finish_kernel, len(merged)),
        in_specs=[pl.BlockSpec(memory_space=pltpu.SMEM)] + [vmem] * (1 + len(merged) + len(inner)),
        out_shape=[
            jax.ShapeDtypeStruct((1, size), F32),
            jax.ShapeDtypeStruct((len(inner), size), F32),
        ],
        scratch_shapes=[square] * 3,
        compiler_params=pltpu.CompilerParams(vmem_limit_bytes=VMEM_BYTES),
        name="finish",
    )(bits, arc, *merged, *inner)


def shards(jac_first, jac_second, residual, damp_inner, damp_sep):
    tiles = lax.psum(gram(jac_first[0], jac_second[0], residual[0]), "band")
    arc, *inner = segment(tiles, damp_inner[0], damp_sep)
    count = lax.axis_size("seg")
    levels = count.bit_length() - 1
    here = lax.axis_index("seg")
    bits = jnp.stack([(here >> level) & 1 for level in range(levels)]).astype(jnp.int32)
    merged = []
    for level in range(levels):
        pairs = [(i, i ^ (1 << level)) for i in range(count)]
        other = lax.ppermute(arc, "seg", pairs)
        arc, saved = merge(bits[level : level + 1], arc, other)
        merged.append(saved)
    sep, steps = finish(bits, arc, merged, inner)
    return (sep, steps[None])


def solution(mesh):
    return jax.shard_map(
        shards,
        mesh=mesh,
        in_specs=(
            P("seg", None, "band", None),
            P("seg", None, "band", None),
            P("seg", None, "band"),
            P("seg", None, None),
            P("seg", None),
        ),
        out_specs=(P("seg", None), P("seg", None, None)),
        check_vma=False,
    )
```

time: 1130 us -> 455 us (0.40)
  other arithmetic: 624 us -> 0.08 us
  Pallas kernels: 0 us -> 145 us
  matrix products: 137 us -> 0 us
  local copies, waits for them, and re-layouts: 71.6 us -> 10.5 us
  waiting for transfers between devices: 220 us -> 276 us
  blocking collectives: 25.7 us -> 0 us
  between operations: 30.5 us -> 14.5 us
    another operation x101 -> x1, other arithmetic: 610 us -> 0.08 us  [shards(): jnp.stack([here >> level & 1 for level in range(levels)]).astype(jnp.int32)]
    pallas_call x0 -> x6, Pallas kernels: none -> 145 us  [the longest x3 62.1 us: merge(): pl.pallas_call(merge_kernel, in_specs=[pl.BlockSpec(memory_space=pltpu.SM...]
    dot_general x37 -> x0, matrix products: 74.9 us -> none  [the longest x32 55.3 us: matmul_high(): return jnp.matmul(left, right, precision=HIGH)]
    another operation x153 -> x0, matrix products: 62.6 us -> none  [the longest x30 18.8 us: merge(): weights = jax.scipy.linalg.cho_solve((chol, True), couple)]
    another operation x92 -> x0, local copies, waits for them, and re-layouts: 43 us -> none  [the longest x35 18.5 us: lower_solve(): return jax.scipy.linalg.solve_triangular(chol, rhs, lower=True)]
    psum x1, waiting for transfers between devices: 164 us -> 194 us  [shards(): tiles = lax.psum(gram(jac_first[0], jac_second[0], residual[0]), 'band')]
    ppermute x16 -> x3, waiting for transfers between devices: 55.5 us -> 82.1 us  [shards(): other = lax.ppermute(arc, 'seg', pairs)]
    psum x1 -> x0, blocking collectives: 25.7 us -> none  [shards(): diag, off, grad = lax.psum((diag_part, off_part, grad_part), 'band')]
  transfers between devices with their start and end apart: 17 -> 4, of which waited for: 7 -> 4; matrix products, arithmetic and copies ran while one was open for 31% -> 0% of each run, Pallas kernels for 0% -> 0%
where the time goes in v1:
time: 455 us; the launch traced here: 449 us
  waiting for transfers between devices  276 us (61%)
  Pallas kernels  145 us (32%)
  between operations  14.5 us (3%)
  local copies, waits for them, and re-layouts  10.5 us (2%)
    psum x1, waiting for transfers between devices, shards(): tiles = lax.psum(gram(jac_first[0], jac_second[0], residual[0]), 'band')  194 us
    ppermute x3, waiting for transfers between devices, shards(): other = lax.ppermute(arc, 'seg', pairs)  82.1 us
    pallas_call x3, Pallas kernels, merge(): pl.pallas_call(merge_kernel, in_specs=[pl.BlockSpec(memory_space=pltpu.SM...  62.1 us
    pallas_call x1, Pallas kernels, segment(): pl.pallas_call(segment_kernel, out_shape=[jax.ShapeDtypeStruct((3 * size...  54.2 us
    pallas_call x1, Pallas kernels, finish(): pl.pallas_call(functools.partial(finish_kernel, len(merged)), in_specs=[p...  17.7 us
    pallas_call x1, Pallas kernels, gram(): pl.pallas_call(functools.partial(gram_kernel, links=links, size=size), gr...  10.5 us
    unnamed x26, local copies, waits for them, and re-layouts  9.83 us
  transfers between devices with their start and end apart: 4, of which 4 were waited for; matrix products, arithmetic and copies ran while one was open for 0% of the time, Pallas kernels for 0%

profile of v1, /device:TPU:0, one launch (start us, length us, event | category | flops | bytes accessed | tf_op | source)
XLA Modules:
  0.0 448.7 jit_solution(17948899132217905525)
XLA Ops:
  7.2 0.0 all-reduce.2.cloned.1.call-start
  7.2 0.7 broadcast_in_dim.11.resid_ref
  7.9 0.0 copy-start
  7.9 1.9 copy-done
  9.8 10.5 %gram.1 = f32[3464,384]{1,0:T(8,128)} custom-call(bf16[4,1024,384]{2,1,0:T(8,128)(2,1)S(1)} %bitcast.10, bf16[4,1024,384]{2,1,0:T(8,128)(2,1)} %bitcast.13, bf16[4,16,1024]{2,1,0:T(8,128)(2,1)S(1)} %broadcast_in_dim.11.resid_ref), custom_call_target="tpu_custom_call" | custom-call | tf_op jit(solution)/shard_map/gram/pallas_call | solution.py:151
  20.4 0.0 all-reduce.2.cloned.1.call-update
  20.4 0.7 copy-done.11
  21.1 193.9 %all-reduce.2.cloned.1.call-done.tiles_ref = f32[3464,384]{1,0:T(8,128)} async-done(((f32[3464,384]{1,0:T(8,128)}), f32[3464,384]{1,0:T(8,128)}) %all-reduce.2.cloned.1.call-update) | async-done | bytes 5320720 | tf_op jit(solution)/shard_map/psum | solution.py:307
  214.9 0.0 copy-done.9
  214.9 54.2 %segment.1 = (f32[1160,384]{1,0:T(8,128)S(1)}, f32[776,384]{1,0:T(8,128)S(1)}, f32[776,384]{1,0:T(8,128)S(1)}, f32[776,384]{1,0:T(8,128)S(1)}) custom-call(f32[3464,384]{1,0:T(8,128)} %all-reduce.2.cloned.1.call-done.tiles_ref, f32[3,384]{1,0:T(4,128)S(1)} %bitcast.11, f32[1,384]{1,0:T(1,128)S(1)} %copy-done.9), custom_call_target="tpu_custom_call" | custom-call | tf_op jit(solution)/shard_map/segment/pallas_call | solution.py:201
  269.1 1.1 copy-done.2
  270.2 1.0 copy-done.4
  271.2 0.0 collective-permute-start
  271.2 3.8 collective-permute-done.other_ref
  275.1 21.5 %merge.3 = (f32[1160,384]{1,0:T(8,128)}, f32[776,384]{1,0:T(8,128)S(1)}) custom-call(s32[1]{0:T(128)} %bitcast.right_ref, f32[1160,384]{1,0:T(8,128)S(1)} %get-tuple-element.14.mine_ref, f32[1160,384]{1,0:T(8,128)} %collective-permute-done.other_ref), custom_call_target="tpu_custom_call" | custom-call | tf_op jit(solution)/shard_map/merge/pallas_call | solution.py:243
  296.6 1.0 copy-done.5
  297.6 1.5 collective-permute-start.1
  299.1 39.7 %collective-permute-done.1.other_ref = f32[1160,384]{1,0:T(8,128)S(1)} collective-permute-done((f32[1160,384]{1,0:T(8,128)}, f32[1160,384]{1,0:T(8,128)S(1)}, u32[]{:S(2)}, u32[]{:S(2)}) %collective-permute-start.1) | collective-permute-done | bytes 1781792 | tf_op jit(solution)/shard_map/ppermute | solution.py:316
  338.8 1.2 copy-done.10
  340.0 20.5 %merge.4 = (f32[1160,384]{1,0:T(8,128)S(1)}, f32[776,384]{1,0:T(8,128)S(1)}) custom-call(s32[1]{0:T(128)} %bitcast.1.right_ref, f32[1160,384]{1,0:T(8,128)} %get-tuple-element.15.mine_ref, f32[1160,384]{1,0:T(8,128)} %copy-done.10), custom_call_target="tpu_custom_call" | custom-call | tf_op jit(solution)/shard_map/merge/pallas_call | solution.py:243
  360.5 0.0 copy-start.7
  360.5 1.0 copy-done.7
  361.6 1.5 collective-permute-start.2
  363.0 0.1 pad_add_fusion.bits_ref
  363.1 38.6 %collective-permute-done.2.other_ref = f32[1160,384]{1,0:T(8,128)} collective-permute-done((f32[1160,384]{1,0:T(8,128)S(1)}, f32[1160,384]{1,0:T(8,128)}, u32[]{:S(2)}, u32[]{:S(2)}) %collective-permute-start.2) | collective-permute-done | bytes 1781792 | tf_op jit(solution)/shard_map/ppermute | solution.py:316
  401.8 20.1 %merge.5 = (f32[1160,384]{1,0:T(8,128)S(1)}, f32[776,384]{1,0:T(8,128)S(1)}) custom-call(s32[1]{0:T(128)} %bitcast.2.right_ref, f32[1160,384]{1,0:T(8,128)S(1)} %get-tuple-element.16.mine_ref, f32[1160,384]{1,0:T(8,128)} %collective-permute-done.2.other_ref), custom_call_target="tpu_custom_call" | custom-call | tf_op jit(solution)/shard_map/merge/pallas_call | solution.py:243
  421.8 0.0 copy-start.1
  421.8 1.3 copy-done.1
  423.1 0.0 copy-done.3
  423.1 0.0 copy-done.8
  423.1 17.7 %finish.1 = (f32[1,384]{1,0:T(1,128)}, f32[3,384]{1,0:T(4,128)S(1)}) custom-call(s32[3]{0:T(128)S(1)} %pad_add_fusion.bits_ref, f32[1160,384]{1,0:T(8,128)} %copy-done.1, f32[776,384]{1,0:T(8,128)S(1)} %copy-done.6, f32[776,384]{1,0:T(8,128)S(1)} %copy-done.8, f32[776,384]{1,0:T(8,128)S(1)} %get-tuple-element.20.refs_2_, ...), custom_call_target="tpu_custom_call" | custom-call | tf_op jit(solution)/shard_map/finish/pallas_call | solution.py:293
  440.8 0.6 copy.7
  (11 shorter events, 0.0 us)
Async XLA Ops:
  7.2 207.8 %all-reduce.2.cloned.1.call-start = ((), (), s32[]{:S(2)}) async-start(), calls=%async_computation | async-start | bytes 10641408 | tf_op jit(solution)/shard_map/psum | solution.py:307
  7.9 1.9 copy-start
  20.4 0.7 copy-start.11
  20.4 194.6 %copy-start.9 = (f32[1,384]{1,0:T(1,128)S(1)}, f32[1,384]{1,0:T(1,128)}, u32[]{:S(2)}) copy-start(f32[1,384]{1,0:T(1,128)} %sep_ref.1) | copy-start | bytes 4612
  269.1 1.1 copy-start.2
  270.2 1.0 copy-start.4
  271.2 3.8 collective-permute-start
  296.6 1.0 copy-start.5
  297.6 41.1 %collective-permute-start.1 = (f32[1160,384]{1,0:T(8,128)}, f32[1160,384]{1,0:T(8,128)S(1)}, u32[]{:S(2)}, u32[]{:S(2)}) collective-permute-start(f32[1160,384]{1,0:T(8,128)} %get-tuple-element.15.mine_ref), channel_id=1, source_target_pairs={{0,8},{4,12},{8,0},{12,4},{16,24},{20,28},{24,16},{28,20},{1,9},{5... | collective-permute-start | bytes 5345288 | tf_op jit(solution)/shard_map/ppermute | solution.py:316
  338.7 1.2 copy-start.10
  360.5 1.0 copy-start.7
  361.6 40.2 %collective-permute-start.2 = (f32[1160,384]{1,0:T(8,128)S(1)}, f32[1160,384]{1,0:T(8,128)}, u32[]{:S(2)}, u32[]{:S(2)}) collective-permute-start(f32[1160,384]{1,0:T(8,128)S(1)} %get-tuple-element.16.mine_ref), channel_id=1, source_target_pairs={{0,16},{4,20},{8,24},{12,28},{16,0},{20,4},{24,8},{28,12},{1,17},{... | collective-permute-start | bytes 5345288 | tf_op jit(solution)/shard_map/ppermute | solution.py:316
  363.1 60.0 %copy-start.3 = (f32[776,384]{1,0:T(8,128)S(1)}, f32[776,384]{1,0:T(8,128)}, u32[]{:S(2)}) copy-start(f32[776,384]{1,0:T(8,128)} %copy-done.2) | copy-start | bytes 3575812
  363.1 60.0 %copy-start.6 = (f32[776,384]{1,0:T(8,128)S(1)}, f32[776,384]{1,0:T(8,128)}, u32[]{:S(2)}) copy-start(f32[776,384]{1,0:T(8,128)} %copy-done.5) | copy-start | bytes 3575812
  363.1 60.0 %copy-start.8 = (f32[776,384]{1,0:T(8,128)S(1)}, f32[776,384]{1,0:T(8,128)}, u32[]{:S(2)}) copy-start(f32[776,384]{1,0:T(8,128)} %copy-done.7) | copy-start | bytes 3575812
  421.8 1.3 copy-start.1
Sparse Core Ops, SparseCore 0:
  20.5 194.3 all-reduce.1
